TPU v7x, 256 devices: a whole 4x4x8 slice. The times are simulated.
256 devices in a mesh: gx: 16 (over y_hi, z), gy: 16 (over y_lo, x, core).
Axes of the slice: x: 4, y: 4 (y_hi: 2, y_lo: 2; y = y_hi * 2 + y_lo), z: 8, core: 2. Of those that a mesh axis runs over, the one named last changes fastest.
Arguments:
- input_field: bfloat16 [64, 64, 128, 128], P(None, 'gx', 'gy'), may hold values from -6 to 6
- first_weight: bfloat16 [3, 3, 3, 64, 64], replicated, may hold values from -0.15625 to 0.15625
- first_bias: float32 [64], replicated, may hold values from -3 to 3
- down_weight: bfloat16 [2, 2, 2, 128, 64], replicated, may hold values from -0.25 to 0.25
- down_bias: float32 [128], replicated, may hold values from -3 to 3
- second_weight: bfloat16 [3, 3, 3, 128, 128], replicated, may hold values from -0.109375 to 0.109375
- second_bias: float32 [128], replicated, may hold values from -3 to 3
- third_weight: bfloat16 [3, 3, 3, 128, 128], replicated, may hold values from -0.109375 to 0.109375
- third_bias: float32 [128], replicated, may hold values from -3 to 3
- up_weight: bfloat16 [2, 2, 2, 64, 128], replicated, may hold values from -0.5 to 0.5
- up_bias: float32 [64], replicated, may hold values from -3 to 3
- last_weight: bfloat16 [3, 3, 3, 64, 64], replicated, may hold values from -0.15625 to 0.15625
- last_bias: float32 [64], replicated, may hold values from -3 to 3
Outputs:
- output_field: bfloat16 [64, 64, 128, 128], P(None, 'gx', 'gy')
All inputs are finite; a program needn't handle non-finite values.
Results may differ from a plain program's by a relative error of at most 0.009.
Values may be sent and summed in bfloat16 or wider, within the bound.
A program may use at most 64 MiB of HBM per device.

v0:
```python
import jax
import jax.numpy as jnp
from jax import lax
from jax.sharding import PartitionSpec as P


def with_halo(array, sides, width):
    for axis, dim in sides:
        size, length = (lax.axis_size(axis), array.shape[dim])
        up = [(i, (i + 1) % size) for i in range(size)]
        down = [(j, i) for i, j in up]
        last = lax.slice_in_dim(array, length - width, length, axis=dim)
        initial = lax.slice_in_dim(array, 0, width, axis=dim)
        before = lax.ppermute(last, axis, up)
        after = lax.ppermute(initial, axis, down)
        array = jnp.concatenate([before, array, after], axis=dim)
    return array


def leaky_unit(values):
    return jnp.where(values > 0, values, 0.2 * values)


def column(bias):
    return bias[:, None, None, None]


def valid_conv(padded, weight):
    rolled = jnp.stack([jnp.roll(padded, 1 - shift_z, axis=3) for shift_z in range(3)])
    width_out = padded.shape[1] - 2
    height_out = padded.shape[2] - 2
    summed = jnp.zeros((weight.shape[3], width_out, height_out, padded.shape[3]), jnp.float32)
    for shift_x in range(3):
        for shift_y in range(3):
            window = rolled[:, :, shift_x : shift_x + width_out, shift_y : shift_y + height_out]
            summed = summed + jnp.einsum(
                "koc,kcxyz->oxyz",
                weight[shift_x, shift_y],
                window,
                preferred_element_type=jnp.float32,
            )
    return summed


def shrink(field, weight):
    chans, wide_x, wide_y, wide_z = field.shape
    blocks = field.reshape(chans, wide_x // 2, 2, wide_y // 2, 2, wide_z // 2, 2)
    return jnp.einsum("pqroc,cipjqkr->oijk", weight, blocks, preferred_element_type=jnp.float32)


def expand(field, weight):
    chans, wide_x, wide_y, wide_z = field.shape
    spread = jnp.einsum("pqroc,cijk->oipjqkr", weight, field, preferred_element_type=jnp.float32)
    return spread.reshape(weight.shape[3], 2 * wide_x, 2 * wide_y, 2 * wide_z)


def body(
    input_field,
    first_weight,
    first_bias,
    down_weight,
    down_bias,
    second_weight,
    second_bias,
    third_weight,
    third_bias,
    up_weight,
    up_bias,
    last_weight,
    last_bias,
):
    padded = with_halo(input_field, (("gx", 1), ("gy", 2)), 1)
    skip = leaky_unit(valid_conv(padded, first_weight) + column(first_bias)).astype(jnp.bfloat16)
    coarse = leaky_unit(shrink(skip, down_weight) + column(down_bias)).astype(jnp.bfloat16)
    coarse_pad = with_halo(coarse, (("gx", 1), ("gy", 2)), 1)
    middle_core = leaky_unit(valid_conv(coarse_pad, second_weight) + column(second_bias)).astype(
        jnp.bfloat16
    )
    middle = with_halo(middle_core, (("gx", 1), ("gy", 2)), 1)
    final_coarse = (
        coarse.astype(jnp.float32)
        + leaky_unit(valid_conv(middle, third_weight) + column(third_bias))
    ).astype(jnp.bfloat16)
    lifted = expand(final_coarse, up_weight)
    merged_core = (leaky_unit(lifted + column(up_bias)) + skip.astype(jnp.float32)).astype(
        jnp.bfloat16
    )
    merged = with_halo(merged_core, (("gx", 1), ("gy", 2)), 1)
    return (valid_conv(merged, last_weight) + column(last_bias)).astype(jnp.bfloat16)


def solution(mesh):
    return jax.shard_map(
        body,
        mesh=mesh,
        in_specs=(
            P(None, "gx", "gy", None),
            P(),
            P(),
            P(),
            P(),
            P(),
            P(),
            P(),
            P(),
            P(),
            P(),
            P(),
            P(),
        ),
        out_specs=P(None, "gx", "gy", None),
        check_vma=False,
    )
```

profile of v0, /device:TPU:7, one launch (start us, length us, event | category | flops | bytes accessed | tf_op | source)
XLA Modules:
  0.0 100.2 jit_solution(9727832910004411134)
XLA Ops:
  1.1 1.7 %collective-permute-start = (bf16[64,1,8,128]{3,0,2,1:T(8,128)(2,1)S(1)}, bf16[64,1,8,128]{3,0,2,1:T(8,128)(2,1)S(1)}, u32[]{:S(2)}, u32[]{:S(2)}) collective-permute-start(bf16[64,1,8,128]{3,0,2,1:T(8,128)(2,1)S(1)} %copy.349), channel_id=1, source_target_pairs={{0,16},{16,32},{32,48},{48,64},{64,80},{80,96},{96,112},{112,128},... | collective-permute-start | bytes 393224 | tf_op jit(solution)/shard_map/ppermute | solution.py:14
  2.8 6.7 %collective-permute-start.1 = (bf16[64,1,8,128]{3,0,2,1:T(8,128)(2,1)S(1)}, bf16[64,1,8,128]{3,0,2,1:T(8,128)(2,1)S(1)}, u32[]{:S(2)}, u32[]{:S(2)}) collective-permute-start(bf16[64,1,8,128]{3,0,2,1:T(8,128)(2,1)S(1)} %copy.350), channel_id=1, source_target_pairs={{16,0},{32,16},{48,32},{64,48},{80,64},{96,80},{112,96},{128,112},... | collective-permute-start | bytes 393224 | tf_op jit(solution)/shard_map/ppermute | solution.py:15
  9.5 3.1 %collective-permute-done = bf16[64,1,8,128]{3,0,2,1:T(8,128)(2,1)S(1)} collective-permute-done((bf16[64,1,8,128]{3,0,2,1:T(8,128)(2,1)S(1)}, bf16[64,1,8,128]{3,0,2,1:T(8,128)(2,1)S(1)}, u32[]{:S(2)}, u32[]{:S(2)}) %collective-permute-start) | collective-permute-done | bytes 131104 | tf_op jit(solution)/shard_map/ppermute | solution.py:14
  12.9 1.5 %collective-permute-start.2 = (bf16[64,6,1,128]{3,0,2,1:T(8,128)(2,1)S(1)}, bf16[64,6,1,128]{3,0,2,1:T(8,128)(2,1)S(1)}, u32[]{:S(2)}, u32[]{:S(2)}) collective-permute-start(bf16[64,6,1,128]{3,0,2,1:T(8,128)(2,1)S(1)} %get-tuple-element.44), channel_id=1, source_target_pairs={{0,1},{1,2},{2,3},{3,4},{4,5},{5,6},{6,7},{7,8},{8,9},{9,10},{10,1... | collective-permute-start | bytes 294920 | tf_op jit(solution)/shard_map/ppermute | solution.py:14
  14.4 1.6 %collective-permute-done.2 = bf16[64,6,1,128]{3,0,2,1:T(8,128)(2,1)S(1)} collective-permute-done((bf16[64,6,1,128]{3,0,2,1:T(8,128)(2,1)S(1)}, bf16[64,6,1,128]{3,0,2,1:T(8,128)(2,1)S(1)}, u32[]{:S(2)}, u32[]{:S(2)}) %collective-permute-start.2) | collective-permute-done | bytes 98336 | tf_op jit(solution)/shard_map/ppermute | solution.py:14
  16.1 4.5 %collective-permute-done.3 = bf16[64,6,1,128]{3,0,2,1:T(8,128)(2,1)S(1)} collective-permute-done((bf16[64,6,1,128]{3,0,2,1:T(8,128)(2,1)S(1)}, bf16[64,6,1,128]{3,0,2,1:T(8,128)(2,1)S(1)}, u32[]{:S(2)}, u32[]{:S(2)}) %collective-permute-start.3) | collective-permute-done | bytes 98336 | tf_op jit(solution)/shard_map/ppermute | solution.py:15
  21.6 1.1 %maximum_bitcast_fusion = (bf16[1,64,6,10,128]{4,1,0,3,2:T(8,128)(2,1)S(1)}, bf16[1,64,6,10,128]{4,1,0,3,2:T(8,128)(2,1)S(1)}) fusion(bf16[64,6,10,127]{3,0,2,1:T(8,128)(2,1)S(1)} %get-tuple-element.38, bf16[64,6,10,1]{3,0,2,1:T(8,128)(2,1)S(1)} %get-tuple-element.36, bf16[64,6,10,1]{3,0,2,1:T(8,128)(2,1)S(1)} %get-tuple-element.37, ...), kind=kLoop, calls=%fused_computation.80 | loop fusion | flops 3932160 | bytes 3932160 | tf_op jit(solution)/shard_map/stack | solution.py:29
  29.7 5.6 %collective-permute-start.5 = (bf16[128,1,4,64]{0,3,2,1:T(8,128)(2,1)S(1)}, bf16[128,1,4,64]{0,3,2,1:T(8,128)(2,1)S(1)}, u32[]{:S(2)}, u32[]{:S(2)}) collective-permute-start(bf16[128,1,4,64]{0,3,2,1:T(8,128)(2,1)S(1)} %get-tuple-element.65), channel_id=1, source_target_pairs={{16,0},{32,16},{48,32},{64,48},{80,64},{96,80},{112,96},{128,112},... | collective-permute-start | bytes 196616 | tf_op jit(solution)/shard_map/ppermute | solution.py:15
  35.3 1.6 %collective-permute-done.4 = bf16[128,1,4,64]{0,3,2,1:T(8,128)(2,1)S(1)} collective-permute-done((bf16[128,1,4,64]{0,3,2,1:T(8,128)(2,1)S(1)}, bf16[128,1,4,64]{0,3,2,1:T(8,128)(2,1)S(1)}, u32[]{:S(2)}, u32[]{:S(2)}) %collective-permute-start.4) | collective-permute-done | bytes 65568 | tf_op jit(solution)/shard_map/ppermute | solution.py:14
  37.6 1.3 %collective-permute-done.6 = bf16[128,4,1,64]{0,3,2,1:T(8,128)(2,1)S(1)} collective-permute-done((bf16[128,4,1,64]{0,3,2,1:T(8,128)(2,1)S(1)}, bf16[128,4,1,64]{0,3,2,1:T(8,128)(2,1)S(1)}, u32[]{:S(2)}, u32[]{:S(2)}) %collective-permute-start.6) | collective-permute-done | bytes 65568 | tf_op jit(solution)/shard_map/ppermute | solution.py:14
  39.0 4.5 %collective-permute-done.7 = bf16[128,4,1,64]{0,3,2,1:T(8,128)(2,1)S(1)} collective-permute-done((bf16[128,4,1,64]{0,3,2,1:T(8,128)(2,1)S(1)}, bf16[128,4,1,64]{0,3,2,1:T(8,128)(2,1)S(1)}, u32[]{:S(2)}, u32[]{:S(2)}) %collective-permute-start.7) | collective-permute-done | bytes 65568 | tf_op jit(solution)/shard_map/ppermute | solution.py:15
  48.1 6.0 %collective-permute-start.9 = (bf16[128,1,4,64]{0,3,2,1:T(8,128)(2,1)S(1)}, bf16[128,1,4,64]{0,3,2,1:T(8,128)(2,1)S(1)}, u32[]{:S(2)}, u32[]{:S(2)}) collective-permute-start(bf16[128,1,4,64]{0,3,2,1:T(8,128)(2,1)S(1)} %get-tuple-element.63), channel_id=1, source_target_pairs={{16,0},{32,16},{48,32},{64,48},{80,64},{96,80},{112,96},{128,112},... | collective-permute-start | bytes 196616 | tf_op jit(solution)/shard_map/ppermute | solution.py:15
  54.1 1.6 %collective-permute-done.8 = bf16[128,1,4,64]{0,3,2,1:T(8,128)(2,1)S(1)} collective-permute-done((bf16[128,1,4,64]{0,3,2,1:T(8,128)(2,1)S(1)}, bf16[128,1,4,64]{0,3,2,1:T(8,128)(2,1)S(1)}, u32[]{:S(2)}, u32[]{:S(2)}) %collective-permute-start.8) | collective-permute-done | bytes 65568 | tf_op jit(solution)/shard_map/ppermute | solution.py:14
  56.3 1.1 %collective-permute-done.10 = bf16[128,4,1,64]{0,3,2,1:T(8,128)(2,1)S(1)} collective-permute-done((bf16[128,4,1,64]{0,3,2,1:T(8,128)(2,1)S(1)}, bf16[128,4,1,64]{0,3,2,1:T(8,128)(2,1)S(1)}, u32[]{:S(2)}, u32[]{:S(2)}) %collective-permute-start.10) | collective-permute-done | bytes 65568 | tf_op jit(solution)/shard_map/ppermute | solution.py:14
  57.4 4.5 %collective-permute-done.11 = bf16[128,4,1,64]{0,3,2,1:T(8,128)(2,1)S(1)} collective-permute-done((bf16[128,4,1,64]{0,3,2,1:T(8,128)(2,1)S(1)}, bf16[128,4,1,64]{0,3,2,1:T(8,128)(2,1)S(1)}, u32[]{:S(2)}, u32[]{:S(2)}) %collective-permute-start.11) | collective-permute-done | bytes 65568 | tf_op jit(solution)/shard_map/ppermute | solution.py:15
  66.7 1.7 %copy.74 = f32[64,2,2,4,2,64,2]{0,6,5,4,3,2,1:T(2,128)S(1)} copy(f32[64,2,2,4,2,64,2]{0,5,6,4,2,3,1:T(8,128)S(1)} %convolution_bitcast_fusion) | data formatting | bytes 2097152 | tf_op jit(solution)/shard_map/pqroc,cijk->oipjqkr/transpose | solution.py:53
  69.1 1.3 %fusion.101 = bf16[64,4,8,128]{3,0,2,1:T(8,128)(2,1)S(1)} fusion(bf16[64,4,8,128]{3,0,2,1:T(8,128)(2,1)} %copy-done.2, f32[64,4,8,128]{3,0,2,1:T(8,128)S(1)} %copy.75, f32[64]{0:T(128)S(1)} %copy-done.9), kind=kLoop, calls=%fused_computation.67 | loop fusion | flops 1835008 | bytes 2097408 | tf_op jit(solution)/shard_map/convert_element_type | solution.py:85
  70.5 6.3 %collective-permute-start.13 = (bf16[64,1,8,128]{3,0,2,1:T(8,128)(2,1)S(1)}, bf16[64,1,8,128]{3,0,2,1:T(8,128)(2,1)S(1)}, u32[]{:S(2)}, u32[]{:S(2)}) collective-permute-start(bf16[64,1,8,128]{3,0,2,1:T(8,128)(2,1)S(1)} %get-tuple-element.47), channel_id=1, source_target_pairs={{16,0},{32,16},{48,32},{64,48},{80,64},{96,80},{112,96},{128,112},... | collective-permute-start | bytes 393224 | tf_op jit(solution)/shard_map/ppermute | solution.py:15
  76.9 2.0 %collective-permute-done.12 = bf16[64,1,8,128]{3,0,2,1:T(8,128)(2,1)S(1)} collective-permute-done((bf16[64,1,8,128]{3,0,2,1:T(8,128)(2,1)S(1)}, bf16[64,1,8,128]{3,0,2,1:T(8,128)(2,1)S(1)}, u32[]{:S(2)}, u32[]{:S(2)}) %collective-permute-start.12) | collective-permute-done | bytes 131104 | tf_op jit(solution)/shard_map/ppermute | solution.py:14
  79.5 1.4 %collective-permute-done.14 = bf16[64,6,1,128]{3,0,2,1:T(8,128)(2,1)S(1)} collective-permute-done((bf16[64,6,1,128]{3,0,2,1:T(8,128)(2,1)S(1)}, bf16[64,6,1,128]{3,0,2,1:T(8,128)(2,1)S(1)}, u32[]{:S(2)}, u32[]{:S(2)}) %collective-permute-start.14) | collective-permute-done | bytes 98336 | tf_op jit(solution)/shard_map/ppermute | solution.py:14
  80.9 4.5 %collective-permute-done.15 = bf16[64,6,1,128]{3,0,2,1:T(8,128)(2,1)S(1)} collective-permute-done((bf16[64,6,1,128]{3,0,2,1:T(8,128)(2,1)S(1)}, bf16[64,6,1,128]{3,0,2,1:T(8,128)(2,1)S(1)}, u32[]{:S(2)}, u32[]{:S(2)}) %collective-permute-start.15) | collective-permute-done | bytes 98336 | tf_op jit(solution)/shard_map/ppermute | solution.py:15
  88.2 5.4 %fusion.233 = (bf16[3,64,4,8,128]{4,1,3,2,0:T(8,128)(2,1)S(1)}, bf16[3,64,4,8,128]{4,1,3,2,0:T(8,128)(2,1)S(1)}, bf16[3,64,4,8,128]{4,1,3,2,0:T(8,128)(2,1)S(1)}...) fusion(bf16[3,64,6,10,128]{4,1,3,2,0:T(8,128)(2,1)S(1)} %pad_ma, ...), kind=kLoop, calls=%fused_computation.245 | loop fusion | bytes 28311552 | tf_op jit(solution)/shard_map/slice | solution.py:35
  97.9 1.1 %fusion.105 = bf16[64,4,8,128]{3,0,2,1:T(8,128)(2,1)S(1)} fusion(f32[64]{0:T(128)S(1)} %copy-done.10, f32[4,8,128,64,1]{2,3,0,1,4:T(8,128)S(1)} %fusion.18, f32[4,8,128,64,1]{2,3,0,1,4:T(8,128)S(1)} %fusion.20, f32[4,8,128,64,1]{2,3,0,1,4:T(8,128)S(1)} %fusion.22, f32[4,8,128,64,1]{2,3,0,1,4:T(8,128)S(1)} %fusion.24, f32[4,8,128,64,1]{2,3,0,1,4:T(8,128)S(1)} %fusion.26, ...), kind=kLoop, calls=%fused_computation.88 | loop fusion | flops 2621440 | bytes 9961728 | tf_op jit(solution)/shard_map/convert_element_type | solution.py:89
  99.0 1.1 %copy.85 = bf16[64,4,8,128]{3,2,1,0:T(8,128)(2,1)} copy(bf16[64,4,8,128]{3,0,2,1:T(8,128)(2,1)S(1)} %fusion.105) | data formatting | bytes 1048576 | tf_op jit(solution)/shard_map/convert_element_type | solution.py:89
  (125 shorter events, 28.1 us)
Async XLA Ops:
  0.0 66.2 %copy-start = (bf16[2,2,2,64,128]{4,3,2,1,0:T(8,128)(2,1)S(1)}, bf16[2,2,2,64,128]{4,3,2,1,0:T(8,128)(2,1)}, u32[]{:S(2)}) copy-start(bf16[2,2,2,64,128]{4,3,2,1,0:T(8,128)(2,1)} %param.22) | copy-start | bytes 393220
  0.0 12.6 %copy-start.3 = (bf16[64,4,8,128]{3,2,1,0:T(8,128)(2,1)S(1)}, bf16[64,4,8,128]{3,2,1,0:T(8,128)(2,1)}, u32[]{:S(2)}) copy-start(bf16[64,4,8,128]{3,2,1,0:T(8,128)(2,1)} %param.13) | copy-start | bytes 1572868
  1.1 11.5 %collective-permute-start = (bf16[64,1,8,128]{3,0,2,1:T(8,128)(2,1)S(1)}, bf16[64,1,8,128]{3,0,2,1:T(8,128)(2,1)S(1)}, u32[]{:S(2)}, u32[]{:S(2)}) collective-permute-start(bf16[64,1,8,128]{3,0,2,1:T(8,128)(2,1)S(1)} %copy.349), channel_id=1, source_target_pairs={{0,16},{16,32},{32,48},{48,64},{64,80},{80,96},{96,112},{112,128},... | collective-permute-start | bytes 393224 | tf_op jit(solution)/shard_map/ppermute | solution.py:14
  2.8 10.0 %collective-permute-start.1 = (bf16[64,1,8,128]{3,0,2,1:T(8,128)(2,1)S(1)}, bf16[64,1,8,128]{3,0,2,1:T(8,128)(2,1)S(1)}, u32[]{:S(2)}, u32[]{:S(2)}) collective-permute-start(bf16[64,1,8,128]{3,0,2,1:T(8,128)(2,1)S(1)} %copy.350), channel_id=1, source_target_pairs={{16,0},{32,16},{48,32},{64,48},{80,64},{96,80},{112,96},{128,112},... | collective-permute-start | bytes 393224 | tf_op jit(solution)/shard_map/ppermute | solution.py:15
  12.9 3.1 %collective-permute-start.2 = (bf16[64,6,1,128]{3,0,2,1:T(8,128)(2,1)S(1)}, bf16[64,6,1,128]{3,0,2,1:T(8,128)(2,1)S(1)}, u32[]{:S(2)}, u32[]{:S(2)}) collective-permute-start(bf16[64,6,1,128]{3,0,2,1:T(8,128)(2,1)S(1)} %get-tuple-element.44), channel_id=1, source_target_pairs={{0,1},{1,2},{2,3},{3,4},{4,5},{5,6},{6,7},{7,8},{8,9},{9,10},{10,1... | collective-permute-start | bytes 294920 | tf_op jit(solution)/shard_map/ppermute | solution.py:14
  14.4 6.2 %collective-permute-start.3 = (bf16[64,6,1,128]{3,0,2,1:T(8,128)(2,1)S(1)}, bf16[64,6,1,128]{3,0,2,1:T(8,128)(2,1)S(1)}, u32[]{:S(2)}, u32[]{:S(2)}) collective-permute-start(bf16[64,6,1,128]{3,0,2,1:T(8,128)(2,1)S(1)} %get-tuple-element.45), channel_id=1, source_target_pairs={{1,0},{2,1},{3,2},{4,3},{5,4},{6,5},{7,6},{8,7},{9,8},{10,9},{11,1... | collective-permute-start | bytes 294920 | tf_op jit(solution)/shard_map/ppermute | solution.py:15
  28.1 1.4 %copy-start.2 = (bf16[64,4,8,128]{3,0,2,1:T(8,128)(2,1)}, bf16[64,4,8,128]{3,0,2,1:T(8,128)(2,1)S(1)}, u32[]{:S(2)}) copy-start(bf16[64,4,8,128]{3,0,2,1:T(8,128)(2,1)S(1)} %fusion.95) | copy-start | bytes 1572868
  29.6 7.2 %collective-permute-start.4 = (bf16[128,1,4,64]{0,3,2,1:T(8,128)(2,1)S(1)}, bf16[128,1,4,64]{0,3,2,1:T(8,128)(2,1)S(1)}, u32[]{:S(2)}, u32[]{:S(2)}) collective-permute-start(bf16[128,1,4,64]{0,3,2,1:T(8,128)(2,1)S(1)} %get-tuple-element.64), channel_id=1, source_target_pairs={{0,16},{16,32},{32,48},{48,64},{64,80},{80,96},{96,112},{112,128},... | collective-permute-start | bytes 196616 | tf_op jit(solution)/shard_map/ppermute | solution.py:14
  29.7 7.2 %collective-permute-start.5 = (bf16[128,1,4,64]{0,3,2,1:T(8,128)(2,1)S(1)}, bf16[128,1,4,64]{0,3,2,1:T(8,128)(2,1)S(1)}, u32[]{:S(2)}, u32[]{:S(2)}) collective-permute-start(bf16[128,1,4,64]{0,3,2,1:T(8,128)(2,1)S(1)} %get-tuple-element.65), channel_id=1, source_target_pairs={{16,0},{32,16},{48,32},{64,48},{80,64},{96,80},{112,96},{128,112},... | collective-permute-start | bytes 196616 | tf_op jit(solution)/shard_map/ppermute | solution.py:15
  36.8 2.1 %collective-permute-start.6 = (bf16[128,4,1,64]{0,3,2,1:T(8,128)(2,1)S(1)}, bf16[128,4,1,64]{0,3,2,1:T(8,128)(2,1)S(1)}, u32[]{:S(2)}, u32[]{:S(2)}) collective-permute-start(bf16[128,4,1,64]{0,3,2,1:T(8,128)(2,1)S(1)} %get-tuple-element.60), channel_id=1, source_target_pairs={{0,1},{1,2},{2,3},{3,4},{4,5},{5,6},{6,7},{7,8},{8,9},{9,10},{10,1... | collective-permute-start | bytes 196616 | tf_op jit(solution)/shard_map/ppermute | solution.py:14
  37.6 5.8 %collective-permute-start.7 = (bf16[128,4,1,64]{0,3,2,1:T(8,128)(2,1)S(1)}, bf16[128,4,1,64]{0,3,2,1:T(8,128)(2,1)S(1)}, u32[]{:S(2)}, u32[]{:S(2)}) collective-permute-start(bf16[128,4,1,64]{0,3,2,1:T(8,128)(2,1)S(1)} %get-tuple-element.61), channel_id=1, source_target_pairs={{1,0},{2,1},{3,2},{4,3},{5,4},{6,5},{7,6},{8,7},{9,8},{10,9},{11,1... | collective-permute-start | bytes 196616 | tf_op jit(solution)/shard_map/ppermute | solution.py:15
  44.1 1.2 %copy-start.4 = (bf16[3,3,3,128,128]{4,3,2,1,0:T(8,128)(2,1)S(1)}, bf16[3,3,3,128,128]{4,3,2,1,0:T(8,128)(2,1)}, u32[]{:S(2)}) copy-start(bf16[3,3,3,128,128]{4,3,2,1,0:T(8,128)(2,1)} %param.18) | copy-start | bytes 2654212
  48.0 7.7 %collective-permute-start.8 = (bf16[128,1,4,64]{0,3,2,1:T(8,128)(2,1)S(1)}, bf16[128,1,4,64]{0,3,2,1:T(8,128)(2,1)S(1)}, u32[]{:S(2)}, u32[]{:S(2)}) collective-permute-start(bf16[128,1,4,64]{0,3,2,1:T(8,128)(2,1)S(1)} %get-tuple-element.62), channel_id=1, source_target_pairs={{0,16},{16,32},{32,48},{48,64},{64,80},{80,96},{96,112},{112,128},... | collective-permute-start | bytes 196616 | tf_op jit(solution)/shard_map/ppermute | solution.py:14
  48.1 7.6 %collective-permute-start.9 = (bf16[128,1,4,64]{0,3,2,1:T(8,128)(2,1)S(1)}, bf16[128,1,4,64]{0,3,2,1:T(8,128)(2,1)S(1)}, u32[]{:S(2)}, u32[]{:S(2)}) collective-permute-start(bf16[128,1,4,64]{0,3,2,1:T(8,128)(2,1)S(1)} %get-tuple-element.63), channel_id=1, source_target_pairs={{16,0},{32,16},{48,32},{64,48},{80,64},{96,80},{112,96},{128,112},... | collective-permute-start | bytes 196616 | tf_op jit(solution)/shard_map/ppermute | solution.py:15
  55.7 1.7 %collective-permute-start.10 = (bf16[128,4,1,64]{0,3,2,1:T(8,128)(2,1)S(1)}, bf16[128,4,1,64]{0,3,2,1:T(8,128)(2,1)S(1)}, u32[]{:S(2)}, u32[]{:S(2)}) collective-permute-start(bf16[128,4,1,64]{0,3,2,1:T(8,128)(2,1)S(1)} %get-tuple-element.58), channel_id=1, source_target_pairs={{0,1},{1,2},{2,3},{3,4},{4,5},{5,6},{6,7},{7,8},{8,9},{9,10},{10,1... | collective-permute-start | bytes 196616 | tf_op jit(solution)/shard_map/ppermute | solution.py:14
  56.1 5.8 %collective-permute-start.11 = (bf16[128,4,1,64]{0,3,2,1:T(8,128)(2,1)S(1)}, bf16[128,4,1,64]{0,3,2,1:T(8,128)(2,1)S(1)}, u32[]{:S(2)}, u32[]{:S(2)}) collective-permute-start(bf16[128,4,1,64]{0,3,2,1:T(8,128)(2,1)S(1)} %get-tuple-element.59), channel_id=1, source_target_pairs={{1,0},{2,1},{3,2},{4,3},{5,4},{6,5},{7,6},{8,7},{9,8},{10,9},{11,1... | collective-permute-start | bytes 196616 | tf_op jit(solution)/shard_map/ppermute | solution.py:15
  62.6 1.2 %copy-start.5 = (bf16[3,3,3,128,128]{4,3,2,1,0:T(8,128)(2,1)S(1)}, bf16[3,3,3,128,128]{4,3,2,1,0:T(8,128)(2,1)}, u32[]{:S(2)}) copy-start(bf16[3,3,3,128,128]{4,3,2,1,0:T(8,128)(2,1)} %param.20) | copy-start | bytes 2654212
  65.1 1.1 %copy-start.8 = (f32[128]{0:T(128)S(1)}, f32[128]{0:T(128)}, u32[]{:S(2)}) copy-start(f32[128]{0:T(128)} %param.21) | copy-start | bytes 1540
  70.4 8.5 %collective-permute-start.12 = (bf16[64,1,8,128]{3,0,2,1:T(8,128)(2,1)S(1)}, bf16[64,1,8,128]{3,0,2,1:T(8,128)(2,1)S(1)}, u32[]{:S(2)}, u32[]{:S(2)}) collective-permute-start(bf16[64,1,8,128]{3,0,2,1:T(8,128)(2,1)S(1)} %get-tuple-element.46), channel_id=1, source_target_pairs={{0,16},{16,32},{32,48},{48,64},{64,80},{80,96},{96,112},{112,128},... | collective-permute-start | bytes 393224 | tf_op jit(solution)/shard_map/ppermute | solution.py:14
  70.5 8.4 %collective-permute-start.13 = (bf16[64,1,8,128]{3,0,2,1:T(8,128)(2,1)S(1)}, bf16[64,1,8,128]{3,0,2,1:T(8,128)(2,1)S(1)}, u32[]{:S(2)}, u32[]{:S(2)}) collective-permute-start(bf16[64,1,8,128]{3,0,2,1:T(8,128)(2,1)S(1)} %get-tuple-element.47), channel_id=1, source_target_pairs={{16,0},{32,16},{48,32},{64,48},{80,64},{96,80},{112,96},{128,112},... | collective-permute-start | bytes 393224 | tf_op jit(solution)/shard_map/ppermute | solution.py:15
  78.9 2.0 %collective-permute-start.14 = (bf16[64,6,1,128]{3,0,2,1:T(8,128)(2,1)S(1)}, bf16[64,6,1,128]{3,0,2,1:T(8,128)(2,1)S(1)}, u32[]{:S(2)}, u32[]{:S(2)}) collective-permute-start(bf16[64,6,1,128]{3,0,2,1:T(8,128)(2,1)S(1)} %get-tuple-element.42), channel_id=1, source_target_pairs={{0,1},{1,2},{2,3},{3,4},{4,5},{5,6},{6,7},{7,8},{8,9},{9,10},{10,1... | collective-permute-start | bytes 294920 | tf_op jit(solution)/shard_map/ppermute | solution.py:14
  79.3 6.2 %collective-permute-start.15 = (bf16[64,6,1,128]{3,0,2,1:T(8,128)(2,1)S(1)}, bf16[64,6,1,128]{3,0,2,1:T(8,128)(2,1)S(1)}, u32[]{:S(2)}, u32[]{:S(2)}) collective-permute-start(bf16[64,6,1,128]{3,0,2,1:T(8,128)(2,1)S(1)} %get-tuple-element.43), channel_id=1, source_target_pairs={{1,0},{2,1},{3,2},{4,3},{5,4},{6,5},{7,6},{8,7},{9,8},{10,9},{11,1... | collective-permute-start | bytes 294920 | tf_op jit(solution)/shard_map/ppermute | solution.py:15
  88.2 5.4 %copy-start.6 = (bf16[3,3,3,64,64]{4,3,2,1,0:T(8,128)(2,1)S(1)}, bf16[3,3,3,64,64]{4,3,2,1,0:T(8,128)(2,1)}, u32[]{:S(2)}) copy-start(bf16[3,3,3,64,64]{4,3,2,1,0:T(8,128)(2,1)} %param.24) | copy-start | bytes 663556
  97.9 2.3 %copy-start.1 = (bf16[2,2,2,64,128]{4,3,2,1,0:T(8,128)(2,1)S(1)}, bf16[2,2,2,64,128]{4,3,2,1,0:T(8,128)(2,1)}, u32[]{:S(2)}) copy-start(bf16[2,2,2,64,128]{4,3,2,1,0:T(8,128)(2,1)} %param.22) | copy-start | bytes 393220
  (7 other events, 6.2 us)
where the time goes:
time: 100 us
  waiting for transfers between devices  31.7 us (32%)
  starting transfers between devices  30.1 us (30%)
  local copies, waits for them, and re-layouts  16.9 us (17%)
  matrix products  13.7 us (14%)
  other arithmetic  6.97 us (7%)
    ppermute x8, starting transfers between devices, with_halo(): after = lax.ppermute(initial, axis, down)  25.1 us
    ppermute x8, waiting for transfers between devices, with_halo(): after = lax.ppermute(initial, axis, down)  18 us
    ppermute x8, waiting for transfers between devices, with_halo(): before = lax.ppermute(last, axis, up)  13.7 us
    dot_general x36, matrix products, valid_conv(): jnp.einsum('koc,kcxyz->oxyz', weight[shift_x, shift_y], window, preferred...  12.9 us
    slice x3, local copies, waits for them, and re-layouts, valid_conv(): rolled[:, :, shift_x:shift_x + width_out, shift_y:shift_y + height_out]  7.2 us
    ppermute x8, starting transfers between devices, with_halo(): before = lax.ppermute(last, axis, up)  4.95 us
    another operation x15, other arithmetic, valid_conv(): jnp.stack([jnp.roll(padded, 1 - shift_z, axis=3) for shift_z in range(3)])  3.92 us
    unnamed x34, local copies, waits for them, and re-layouts  2.48 us
  transfers between devices with their start and end apart: 16, of which 12 were waited for; matrix products, arithmetic and copies ran while one was open for 0% of the time, Pallas kernels for 0%

commit v1 on v0

v1 whole, which is shorter than its diff:
```python
import functools

import jax
import jax.numpy as jnp
from jax import lax
from jax.experimental import pallas as pl
from jax.experimental.pallas import tpu as pltpu
from jax.sharding import PartitionSpec as P

BF16 = jnp.bfloat16
F32 = jnp.float32
MESH = pl.DeviceIdType.MESH

C1 = 64
C2 = 128
NZ = 128
HALF = NZ // 2
FX, FY = 4, 8
CX, CY = 2, 4
WAYS = ((1, 0), (-1, 0), (0, 1), (0, -1), (1, 1), (1, -1), (-1, 1), (-1, -1))
FACES_X = ((1, 0), (-1, 0))
FACES_Y = ((0, 1), (0, -1))
CORNERS = WAYS[4:]
IN, COARSE, SKIP, FINAL = range(4)


def leaky(values):
    return jnp.maximum(values, 0.2 * values)


def nn(a, b):
    return lax.dot_general(a, b, (((1,), (0,)), ((), ())), preferred_element_type=F32)


def nt(a, b):
    return lax.dot_general(a, b, (((1,), (1,)), ((), ())), preferred_element_type=F32)


def lanes(parts):
    return jnp.concatenate(parts, axis=1)


def rows(parts):
    return jnp.concatenate(parts, axis=0)


def span(step, size):
    return {1: (size, 0, 1), -1: (1, size + 1, 1), 0: (1, 1, size)}[step]


def kernel(
    nx,
    ny,
    x_hbm,
    w1_hbm,
    wd_hbm,
    w2_hbm,
    w3_hbm,
    wu_hbm,
    w4_hbm,
    b1_hbm,
    bd_hbm,
    b2_hbm,
    b3_hbm,
    bu_hbm,
    b4_hbm,
    out,
    xin,
    beside,
    flat,
    beside_flat,
    acc,
    fine,
    skip,
    merged,
    coarse,
    middle,
    final,
    w1,
    w4,
    wd,
    w2,
    w3,
    wu,
    big1,
    big4,
    edge1,
    edge4,
    b1,
    bd,
    b2,
    b3,
    bu,
    b4,
    col,
    turned2,
    turned3,
    mine,
    third,
    send_sem,
    recv_sem,
    load_sem,
):
    gx, gy = lax.axis_index("gx"), lax.axis_index("gy")

    def device(way):
        return (lax.rem(gx + way[0] + nx, nx), lax.rem(gy + way[1] + ny, ny))

    late_front = lax.rem(gx, nx // 2) == 0

    def each_side(body):
        for late, order in ((True, (1, 0)), (False, (0, 1))):

            @pl.when(late_front if late else jnp.logical_not(late_front))
            def _():
                for k, side in enumerate(order):
                    body(side, k == 0)

    barrier = pltpu.get_barrier_semaphore()
    for way in WAYS:
        pl.semaphore_signal(barrier, inc=1, device_id=device(way), device_id_type=MESH)

    pairs = (
        (x_hbm, xin),
        (w1_hbm, w1),
        (b1_hbm, b1),
        (w4_hbm, w4),
        (wd_hbm, wd),
        (bd_hbm, bd),
        (w2_hbm, w2),
        (b2_hbm, b2),
        (w3_hbm, w3),
        (b3_hbm, b3),
        (wu_hbm, wu),
        (bu_hbm, bu),
        (b4_hbm, b4),
    )
    loads = [pltpu.make_async_copy(s, d, load_sem.at[k]) for k, (s, d) in enumerate(pairs)]
    for load in loads:
        load.start()
    def loaded(*refs):
        for load, (_, ref) in zip(loads, pairs):
            if any(ref is r for r in refs):
                load.wait()

    loaded(xin)
    pl.semaphore_wait(barrier, len(WAYS))

    face_moves = [
        pltpu.make_async_remote_copy(
            src_ref=xin.at[:, (FX - 1) * (1 - side)],
            dst_ref=beside.at[side],
            send_sem=send_sem.at[IN, side],
            recv_sem=recv_sem.at[IN, side],
            device_id=device(FACES_X[side]),
            device_id_type=MESH,
        )
        for side in range(2)
    ]
    for move in face_moves:
        move.start()

    def piece(buffer, phase, slot, way, xs, ys):
        return pltpu.make_async_remote_copy(
            src_ref=buffer.at[pl.ds(xs[0], xs[2]), pl.ds(ys[0], ys[2])],
            dst_ref=buffer.at[pl.ds(xs[1], xs[2]), pl.ds(ys[1], ys[2])],
            send_sem=send_sem.at[phase, slot],
            recv_sem=recv_sem.at[phase, slot],
            device_id=device(way),
            device_id_type=MESH,
        )

    def copies(buffer, phase, wide, high, chunks):
        made = {}
        for k, way in enumerate(WAYS):
            xs, ys = span(way[0], wide), span(way[1], high)
            if way in FACES_X:
                made[way] = [
                    piece(buffer, phase, 8 + 4 * k + c, way, xs, (1 + first, 1 + first, count))
                    for c, (first, count) in enumerate(chunks)
                ]
            else:
                made[way] = [piece(buffer, phase, k, way, xs, ys)]
        return made

    moves = {
        SKIP: copies(skip, SKIP, FX, FY, [(0, FY // 2), (FY // 2, FY // 2)]),
        FINAL: copies(final, FINAL, CX, CY, [(0, CY)]),
    }
    def double(step, size):
        return {1: (size, 0, 2), -1: (2, size + 2, 2), 0: (2, 2, size)}[step]

    moves[COARSE] = {
        way: [piece(coarse, COARSE, k, way, double(way[0], CX), double(way[1], CY))]
        for k, way in enumerate(WAYS)
    }
    moves[IN] = {
        way: [piece(fine, IN, k, way, span(way[0], FX), span(way[1], FY))]
        for k, way in enumerate(WAYS)
        if k >= 2
    }
    for side in range(2):
        moves[IN][FACES_X[side]] = [face_moves[side]]

    def start(phase, ways=WAYS, chunks=None):
        for way in ways:
            for k, move in enumerate(moves[phase][way]):
                if chunks is None or k in chunks:
                    move.start()

    def arrived(phase, ways):
        for way in ways:
            for move in moves[phase][way]:
                move.wait_recv()

    flat[...] = xin[...].astype(F32).reshape(C1 * FX * FY, NZ)
    columns = [(x, y) for x in range(FX) for y in range(FY)]

    def end(pair):
        return (pair[1] in (0, FY - 1)) + (pair[1] in (0, FY - 1) and pair[0] in (0, FX - 1))

    columns.sort(key=end, reverse=True)
    for k, (x, y) in enumerate(columns):
        tile = flat[pl.ds(x * FY + y, C1, stride=FX * FY), :]
        fine[1 + x, 1 + y] = tile.astype(BF16)
        if k == len(CORNERS) - 1:
            start(IN, CORNERS)
        if k == 2 * FX - 1:
            start(IN, FACES_Y)

    def ways_of(step):
        return [(step, 1), (step, -1), (step, 0)]

    def column(slot, bias):
        square = (C1, C1)
        mask = lax.broadcasted_iota(jnp.int32, square, 0) == lax.broadcasted_iota(
            jnp.int32, square, 1
        )
        kept = jnp.where(mask, jnp.broadcast_to(bias[...], square), 0.0)
        col[slot] = jnp.broadcast_to(jnp.sum(kept, axis=1, keepdims=True), (C1, NZ))

    def arrange(w, big, edge):
        blank = jnp.zeros((C1, C1), BF16)
        for dz in range(3):
            for out_x in range(FX):
                row = (dz * FX + out_x) * C1
                for pair in range(FX * 3 // 2):
                    halves = []
                    for k in (2 * pair, 2 * pair + 1):
                        dx = k // 3 - out_x + 1
                        halves.append(w[dx, k % 3, dz] if 0 <= dx < 3 else blank)
                    big[pl.ds(row, C1), pl.ds(128 * pair, 128)] = lanes(halves)
            for side in range(2):
                row = pl.ds(dz * C1, C1)
                edge[side, row, pl.ds(0, 2 * C1)] = lanes([w[2 * side, 0, dz], w[2 * side, 1, dz]])
                edge[side, row, pl.ds(2 * C1, C1)] = w[2 * side, 2, dz]

    loaded(w1, b1)
    arrange(w1, big1, edge1)
    column(0, b1)

    def turn(part, count):
        return (
            pltpu.roll(part[:count], 1, 1)
            + part[count : 2 * count]
            + pltpu.roll(part[2 * count :], NZ - 1, 1)
        )

    def conv_own(field, big, ys, finish):
        window = [field[pl.ds(1, FX), pl.ds(y, 3)].reshape(FX * 3 * C1, NZ) for y in ys]
        made = nn(big[...], lanes(window))
        for t, y in enumerate(ys):
            total = turn(made[:, NZ * t : NZ * t + NZ], FX * C1)
            for x in range(FX):
                part = total[C1 * x : C1 * (x + 1)]
                if x in (0, FX - 1):
                    acc[y, x // (FX - 1)] = part
                else:
                    finish(x, y, part)

    def conv_edge(field, edge, side, ys, finish):
        window = [field[(FX + 1) * side, pl.ds(y, 3)].reshape(3 * C1, NZ) for y in ys]
        made = nn(edge[side], lanes(window))
        for t, y in enumerate(ys):
            part = acc[y, side] + turn(made[:, NZ * t : NZ * t + NZ], C1)
            finish((FX - 1) * side, y, part)

    def finish_first(x, y, part):
        skip[1 + x, 1 + y] = leaky(part + col[0]).astype(BF16)

    def finish_last(x, y, part):
        flat[pl.ds(x * FY + y, C1, stride=FX * FY), :] = part + col[2]

    def turn_weights(w, turned):
        for dx in range(3):
            for dy in range(3):
                turned[dx, dy] = w[dx, dy].T

    conv_own(fine, big1, (2, 3, 4, 5), finish_first)
    arrived(IN, FACES_Y)
    conv_own(fine, big1, (0, 1, 6, 7), finish_first)

    loaded(wd, bd)
    at_row = lax.broadcasted_iota(jnp.int32, (NZ, NZ), 0)
    at_lane = lax.broadcasted_iota(jnp.int32, (NZ, NZ), 1)
    pick = (at_lane == 2 * lax.rem(at_row, HALF) + at_row // HALF).astype(F32).astype(BF16)
    down = rows([wd[px, py, pz] for pz in range(2) for px in range(2) for py in range(2)])
    def take_side(side, _):
        for move in moves[IN][FACES_X[side]]:
            move.wait_recv()
        beside_flat[side] = beside[side].astype(F32).reshape(C1 * FY, NZ)
        for y in range(FY):
            tile = beside_flat[side, pl.ds(y, C1, stride=FY), :]
            fine[(FX + 1) * side, 1 + y] = tile.astype(BF16)
        arrived(IN, ways_of(1 - 2 * side)[:2])
        conv_edge(fine, edge1, side, range(FY), finish_first)

        split = []
        for j in range(CY):
            block = skip[pl.ds(1 + 2 * side, 2), pl.ds(1 + 2 * j, 2)].reshape(4 * C1, NZ)
            moved = nt(pick, block).astype(BF16)
            split.append(lanes([moved[:HALF], moved[HALF:]]))
        value = leaky(nn(rows(split), down) + bd[...]).astype(BF16)
        coarse[2 + side, pl.ds(2, CY)] = value.reshape(CY, HALF, C2)

    loaded(w2, b2)
    turn_weights(w2, turned2)
    each_side(take_side)
    start(COARSE, CORNERS + FACES_X + FACES_Y)

    def sent(phase):
        for way in WAYS:
            for move in moves[phase][way]:
                move.wait_send()

    def along_z(part):
        return (
            pltpu.roll(part[:, :C2], 1, 0)
            + part[:, C2 : 2 * C2]
            + pltpu.roll(part[:, 2 * C2 :], HALF - 1, 0)
        )

    def taken(field, xs, high):
        return lanes(
            [field[x, pl.ds(dy, high)].reshape(high * HALF, C2) for dy in range(3) for x in xs]
        )

    def weights(turned, xs, outs):
        blank = jnp.zeros((C2, 3 * C2), BF16)
        return rows(
            [
                lanes([turned[x - o + 1, dy] if abs(x - o) <= 1 else blank for o in outs])
                for dy in range(3)
                for x in xs
            ]
        )

    def finish_middle(i, j, part):
        middle[i, j] = leaky(part + b2[...]).astype(BF16)

    def finish_final(i, j, part):
        grown = coarse[2 + i, 2 + j].astype(F32) + leaky(part + b3[...])
        final[1 + i, 1 + j] = grown.astype(BF16)

    def meanwhile():
        start(SKIP, CORNERS)
        start(SKIP, FACES_X)
        start(SKIP, FACES_Y)
        loaded(w3, b3)
        turn_weights(w3, turned3)
        loaded(w4, b4, bu)
        arrange(w4, big4, edge4)
        column(1, bu)
        column(2, b4)

    arrived(COARSE, FACES_Y)
    high = CY + 2
    made = nn(taken(coarse, (2, 3), high), weights(turned2, (2, 3), (2, 3)))
    mine[1] = made[:, : 3 * C2]
    mine[2] = made[:, 3 * C2 :]
    mine[0] = nn(taken(coarse, (2,), high), weights(turned2, (2,), (1,)))
    mine[3] = nn(taken(coarse, (3,), high), weights(turned2, (3,), (4,)))
    meanwhile()

    def ring_side(side, first):
        arrived(COARSE, ways_of(1 - 2 * side))
        xs, outs = ((0, 1), (1, 2)) if side == 0 else ((4, 5), (3, 4))
        made = nn(taken(coarse, xs, high), weights(turned2, xs, outs))
        for k, o in enumerate(outs):
            total = mine[o - 1] + made[:, 3 * C2 * k : 3 * C2 * (k + 1)]
            for j in range(high):
                finish_middle(o - 1, j, along_z(total[j * HALF : (j + 1) * HALF]))
        xs = (2 * side, 2 * side + 1)
        made = nn(taken(middle, xs, CY), weights(turned3, xs, (1, 2)))
        third[...] = made if first else third[...] + made

    each_side(ring_side)
    for i in (1, 0):
        for j in range(CY):
            part = third[pl.ds(j * HALF, HALF), pl.ds(3 * C2 * i, 3 * C2)]
            finish_final(i, j, along_z(part))
        start(FINAL, ways_of(2 * i - 1))
    start(FINAL, FACES_Y)

    loaded(wu)
    at_row = lax.broadcasted_iota(jnp.int32, (2 * HALF, 4 * NZ), 0)
    at_lane = lax.broadcasted_iota(jnp.int32, (2 * HALF, 4 * NZ), 1)
    place = (
        (at_row // HALF == lax.rem(at_lane, 2 * NZ) // NZ)
        & (lax.rem(at_lane, NZ) == 2 * lax.rem(at_row, HALF) + at_lane // (2 * NZ))
    ).astype(F32).astype(BF16)

    def lift(cells, parts):
        wide = []
        for k in range(0, len(cells), 2):
            two = rows([final[i, j] for i, j in cells[k : k + 2]]).T
            spread = nn(two, place).astype(BF16)
            wide.append(rows([spread[:, : 2 * NZ], spread[:, 2 * NZ :]]))
        made = nn(rows([lanes([wu[px, py, 0], wu[px, py, 1]]) for px, py, _ in parts]), lanes(wide))
        for k, (_, _, places) in enumerate(parts):
            for t, spot in enumerate(places):
                if spot is None:
                    continue
                x, y = spot
                value = leaky(made[C1 * k : C1 * (k + 1), NZ * t : NZ * (t + 1)] + col[1])
                merged[x, y] = (value + skip[x, y].astype(F32)).astype(BF16)

    def lift_all(cells, which):
        parts = []
        for px, py in which:
            places = [(2 * i - 1 + px, 2 * j - 1 + py) for i, j in cells]
            parts.append((px, py, [(x, y) if 0 <= y < FY + 2 else None for x, y in places]))
        lift(cells, parts)

    every = [(px, py) for px in range(2) for py in range(2)]
    for i in range(1, 1 + CX):
        lift_all([(i, j) for j in range(1, 1 + CY)], every)
    conv_own(merged, big4, (2, 3, 4, 5), finish_last)
    arrived(SKIP, FACES_Y)
    arrived(FINAL, FACES_Y)
    lift_all([(1, 0), (2, 0)], [(0, 1), (1, 1)])
    lift_all([(1, CY + 1), (2, CY + 1)], [(0, 0), (1, 0)])
    conv_own(merged, big4, (0, 1, 6, 7), finish_last)
    for phase in (IN, COARSE, SKIP):
        sent(phase)
    for side in (1, 0):
        arrived(SKIP, ways_of(1 - 2 * side))
        arrived(FINAL, ways_of(1 - 2 * side))
        i, px = ((0, 1), (CX + 1, 0))[side]
        lift_all([(i, j) for j in range(CY + 2)], [(px, 0), (px, 1)])
        conv_edge(merged, edge4, side, range(FY), finish_last)
    out[...] = flat[...].astype(BF16)
    sent(FINAL)


def body(nx, ny, x, w1, b1, wd, bd, w2, b2, w3, b3, wu, bu, w4, b4):
    count = C1 * FX * FY
    any_space = pl.BlockSpec(memory_space=pl.ANY)
    padded = pltpu.VMEM((FX + 2, FY + 2, C1, NZ), BF16)
    padded_coarse = pltpu.VMEM((CX + 2, CY + 2, HALF, C2), BF16)
    conv = pltpu.VMEM((3, 3, 3, C1, C1), BF16)
    conv_coarse = pltpu.VMEM((3, 3, 3 * C2, C2), BF16)
    turned = pltpu.VMEM((3, 3, C2, 3 * C2), BF16)
    big = pltpu.VMEM((3 * FX * C1, 3 * FX * C1), BF16)
    edge = pltpu.VMEM((2, 3 * C1, 3 * C1), BF16)
    args = (
        x,
        w1,
        jnp.swapaxes(wd, 3, 4),
        w2.reshape(3, 3, 3 * C2, C2),
        w3.reshape(3, 3, 3 * C2, C2),
        wu,
        w4,
        b1.reshape(1, C1),
        bd.reshape(1, C2),
        b2.reshape(1, C2),
        b3.reshape(1, C2),
        bu.reshape(1, C1),
        b4.reshape(1, C1),
    )
    out = pl.pallas_call(
        functools.partial(kernel, nx, ny),
        out_shape=jax.ShapeDtypeStruct((count, NZ), BF16),
        in_specs=[any_space] * 13,
        out_specs=pl.BlockSpec(memory_space=pltpu.VMEM),
        scratch_shapes=[
            pltpu.VMEM((C1, FX, FY, NZ), BF16),
            pltpu.VMEM((2, C1, FY, NZ), BF16),
            pltpu.VMEM((count, NZ), F32),
            pltpu.VMEM((2, C1 * FY, NZ), F32),
            pltpu.VMEM((FY, 2, C1, NZ), F32),
            padded,
            padded,
            padded,
            pltpu.VMEM((CX + 4, CY + 4, HALF, C2), BF16),
            padded_coarse,
            padded_coarse,
            conv,
            conv,
            pltpu.VMEM((2, 2, 2, C1, C2), BF16),
            conv_coarse,
            conv_coarse,
            pltpu.VMEM((2, 2, 2, C1, C2), BF16),
            big,
            big,
            edge,
            edge,
            pltpu.VMEM((1, C1), F32),
            pltpu.VMEM((1, C2), F32),
            pltpu.VMEM((1, C2), F32),
            pltpu.VMEM((1, C2), F32),
            pltpu.VMEM((1, C1), F32),
            pltpu.VMEM((1, C1), F32),
            pltpu.VMEM((3, C1, NZ), F32),
            turned,
            turned,
            pltpu.VMEM((CX + 2, (CY + 2) * HALF, 3 * C2), F32),
            pltpu.VMEM((CY * HALF, CX * 3 * C2), F32),
            pltpu.SemaphoreType.DMA((4, 16)),
            pltpu.SemaphoreType.DMA((4, 16)),
            pltpu.SemaphoreType.DMA((13,)),
        ],
        compiler_params=pltpu.CompilerParams(
            collective_id=0, has_side_effects=True, vmem_limit_bytes=48 * 1024 * 1024
        ),
    )(*(pltpu.with_memory_space_constraint(arg, pltpu.HBM) for arg in args))
    return out.reshape(C1, FX, FY, NZ)


def solution(mesh):
    sharded = P(None, "gx", "gy", None)
    return jax.shard_map(
        functools.partial(body, mesh.shape["gx"], mesh.shape["gy"]),
        mesh=mesh,
        in_specs=(sharded,) + (P(),) * 12,
        out_specs=sharded,
        check_vma=False,
    )
```

time: 100 us -> 39.3 us (0.39)
  the two profiles are of different devices: /device:TPU:7 before, /device:TPU:1 now
where the time goes in v1:
time: 39.3 us; the launch traced here: 39.2 us
  Pallas kernels  38.4 us (98%)
  local copies, waits for them, and re-layouts  0.8 us (2%)
    pallas_call x1, Pallas kernels, body(): pl.pallas_call(functools.partial(kernel, nx, ny), out_shape=jax.ShapeDtyp...  38.4 us
    unnamed x1, local copies, waits for them, and re-layouts  0.8 us

profile of v1, /device:TPU:1, one launch (start us, length us, event | category | flops | bytes accessed | tf_op | source)
XLA Modules:
  0.0 39.2 jit_solution(17696400923919782075)
XLA Ops:
  0.0 38.4 %shard_map.127 = bf16[2048,128]{1,0:T(8,128)(2,1)S(1)} custom-call(bf16[64,4,8,128]{3,2,1,0:T(8,128)(2,1)} %x_hbm.1, bf16[3,3,3,64,64]{4,3,2,1,0:T(8,128)(2,1)} %w1_hbm.1, bf16[2,2,2,64,128]{4,3,2,1,0:T(8,128)(2,1)} %bitcast.13, bf16[3,3,384,128]{3,2,1,0:T(8,128)(2,1)} %bitcast.11, bf16[3,3,384,128]{3,2,1,0:T(8,128)(2,1)} %bitcast.12, ...), custom_call_target="tpu_custom_call" | custom-call | tf_op jit(solution)/shard_map/pallas_call | solution.py:481
  38.4 0.8 %copy.15 = bf16[64,4,8,128]{3,2,1,0:T(8,128)(2,1)} copy(bf16[64,4,8,128]{3,2,1,0:T(8,128)(2,1)S(1)} %bitcast.10) | data formatting | bytes 1048576

commit v2 on v1

--- a/solution.py
+++ b/solution.py
@@ -187,11 +187,13 @@
         SKIP: copies(skip, SKIP, FX, FY, [(0, FY // 2), (FY // 2, FY // 2)]),
         FINAL: copies(final, FINAL, CX, CY, [(0, CY)]),
     }
-    def double(step, size):
-        return {1: (size, 0, 2), -1: (2, size + 2, 2), 0: (2, 2, size)}[step]
-
+    column_x = {1: 0, -1: CX + 2, 0: 2}
+    double_y = {1: (CY, 0, 2), -1: (2, CY + 2, 2), 0: (2, 2, CY)}
     moves[COARSE] = {
-        way: [piece(coarse, COARSE, k, way, double(way[0], CX), double(way[1], CY))]
+        way: [
+            piece(coarse, COARSE, 2 * k + i, way, (2 + i, column_x[way[0]] + i, 1), double_y[way[1]])
+            for i in range(CX)
+        ]
         for k, way in enumerate(WAYS)
     }
     moves[IN] = {
@@ -322,11 +324,11 @@
             split.append(lanes([moved[:HALF], moved[HALF:]]))
         value = leaky(nn(rows(split), down) + bd[...]).astype(BF16)
         coarse[2 + side, pl.ds(2, CY)] = value.reshape(CY, HALF, C2)
+        start(COARSE, CORNERS + FACES_X + FACES_Y, (side,))
 
     loaded(w2, b2)
     turn_weights(w2, turned2)
     each_side(take_side)
-    start(COARSE, CORNERS + FACES_X + FACES_Y)
 
     def sent(phase):
         for way in WAYS:
@@ -390,16 +392,19 @@
             total = mine[o - 1] + made[:, 3 * C2 * k : 3 * C2 * (k + 1)]
             for j in range(high):
                 finish_middle(o - 1, j, along_z(total[j * HALF : (j + 1) * HALF]))
-        xs = (2 * side, 2 * side + 1)
-        made = nn(taken(middle, xs, CY), weights(turned3, xs, (1, 2)))
-        third[...] = made if first else third[...] + made
+        if first:
+            xs = (2 * side, 2 * side + 1)
+            third[...] = nn(taken(middle, xs, CY), weights(turned3, xs, (1, 2)))
+            return
+        for i in (side, 1 - side):
+            xs = (2 * side, 2 * side + 1) if i == side else (1 + side,)
+            made = nn(taken(middle, xs, CY), weights(turned3, xs, (1 + i,)))
+            total = third[:, pl.ds(3 * C2 * i, 3 * C2)] + made
+            for j in range(CY):
+                finish_final(i, j, along_z(total[j * HALF : (j + 1) * HALF]))
+            start(FINAL, ways_of(2 * i - 1))
 
     each_side(ring_side)
-    for i in (1, 0):
-        for j in range(CY):
-            part = third[pl.ds(j * HALF, HALF), pl.ds(3 * C2 * i, 3 * C2)]
-            finish_final(i, j, along_z(part))
-        start(FINAL, ways_of(2 * i - 1))
     start(FINAL, FACES_Y)
 
     loaded(wu)

time: 39.3 us -> 36.3 us (0.924)
  Pallas kernels: 38.4 us -> 35.4 us
    pallas_call x1, Pallas kernels: 38.4 us -> 35.4 us  [body(): pl.pallas_call(functools.partial(kernel, nx, ny), out_shape=jax.ShapeDtyp...]
where the time goes in v2:
time: 36.3 us; the launch traced here: 36.2 us
  Pallas kernels  35.4 us (98%)
  local copies, waits for them, and re-layouts  0.8 us (2%)
    pallas_call x1, Pallas kernels, body(): pl.pallas_call(functools.partial(kernel, nx, ny), out_shape=jax.ShapeDtyp...  35.4 us
    unnamed x1, local copies, waits for them, and re-layouts  0.8 us

profile of v2, /device:TPU:1, one launch (start us, length us, event | category | flops | bytes accessed | tf_op | source)
XLA Modules:
  0.0 36.2 jit_solution(12907277451752832584)
XLA Ops:
  0.0 35.4 %shard_map.127 = bf16[2048,128]{1,0:T(8,128)(2,1)S(1)} custom-call(bf16[64,4,8,128]{3,2,1,0:T(8,128)(2,1)} %x_hbm.1, bf16[3,3,3,64,64]{4,3,2,1,0:T(8,128)(2,1)} %w1_hbm.1, bf16[2,2,2,64,128]{4,3,2,1,0:T(8,128)(2,1)} %bitcast.13, bf16[3,3,384,128]{3,2,1,0:T(8,128)(2,1)} %bitcast.11, bf16[3,3,384,128]{3,2,1,0:T(8,128)(2,1)} %bitcast.12, ...), custom_call_target="tpu_custom_call" | custom-call | tf_op jit(solution)/shard_map/pallas_call | solution.py:486
  35.4 0.8 %copy.15 = bf16[64,4,8,128]{3,2,1,0:T(8,128)(2,1)} copy(bf16[64,4,8,128]{3,2,1,0:T(8,128)(2,1)S(1)} %bitcast.10) | data formatting | bytes 1048576

commit v3 on v2

--- a/solution.py
+++ b/solution.py
@@ -144,6 +144,16 @@
                 load.wait()
 
     loaded(xin)
+    columns = [(x, y) for x in range(FX) for y in range(FY)]
+    columns.sort(key=lambda pair: pair[1] not in (0, FY - 1))
+
+    def turn_input(some):
+        for x, y in some:
+            tile = flat[pl.ds(x * FY + y, C1, stride=FX * FY), :]
+            fine[1 + x, 1 + y] = tile.astype(BF16)
+
+    flat[...] = xin[...].astype(F32).reshape(C1 * FX * FY, NZ)
+    turn_input(columns[: 2 * FX])
     pl.semaphore_wait(barrier, len(WAYS))
 
     face_moves = [
@@ -210,25 +220,14 @@
                 if chunks is None or k in chunks:
                     move.start()
 
-    def arrived(phase, ways):
+    def arrived(phase, ways, chunks=None):
         for way in ways:
-            for move in moves[phase][way]:
-                move.wait_recv()
-
-    flat[...] = xin[...].astype(F32).reshape(C1 * FX * FY, NZ)
-    columns = [(x, y) for x in range(FX) for y in range(FY)]
-
-    def end(pair):
-        return (pair[1] in (0, FY - 1)) + (pair[1] in (0, FY - 1) and pair[0] in (0, FX - 1))
-
-    columns.sort(key=end, reverse=True)
-    for k, (x, y) in enumerate(columns):
-        tile = flat[pl.ds(x * FY + y, C1, stride=FX * FY), :]
-        fine[1 + x, 1 + y] = tile.astype(BF16)
-        if k == len(CORNERS) - 1:
-            start(IN, CORNERS)
-        if k == 2 * FX - 1:
-            start(IN, FACES_Y)
+            for k, move in enumerate(moves[phase][way]):
+                if chunks is None or k in chunks:
+                    move.wait_recv()
+
+    start(IN, CORNERS + FACES_Y)
+    turn_input(columns[2 * FX :])
 
     def ways_of(step):
         return [(step, 1), (step, -1), (step, 0)]
@@ -324,7 +323,8 @@
             split.append(lanes([moved[:HALF], moved[HALF:]]))
         value = leaky(nn(rows(split), down) + bd[...]).astype(BF16)
         coarse[2 + side, pl.ds(2, CY)] = value.reshape(CY, HALF, C2)
-        start(COARSE, CORNERS + FACES_X + FACES_Y, (side,))
+        start(COARSE, ways_of(2 * side - 1) + ways_of(1 - 2 * side), (side,))
+        start(COARSE, FACES_Y, (side,))
 
     loaded(w2, b2)
     turn_weights(w2, turned2)
@@ -385,9 +385,12 @@
     meanwhile()
 
     def ring_side(side, first):
-        arrived(COARSE, ways_of(1 - 2 * side))
-        xs, outs = ((0, 1), (1, 2)) if side == 0 else ((4, 5), (3, 4))
-        made = nn(taken(coarse, xs, high), weights(turned2, xs, outs))
+        far, near, outs = (0, 1, (1, 2)) if side == 0 else (5, 4, (3, 4))
+        arrived(COARSE, ways_of(1 - 2 * side), (side,))
+        o = outs[side]
+        mine[o - 1] = mine[o - 1] + nn(taken(coarse, (far,), high), weights(turned2, (far,), (o,)))
+        arrived(COARSE, ways_of(1 - 2 * side), (1 - side,))
+        made = nn(taken(coarse, (near,), high), weights(turned2, (near,), outs))
         for k, o in enumerate(outs):
             total = mine[o - 1] + made[:, 3 * C2 * k : 3 * C2 * (k + 1)]
             for j in range(high):

time: 36.3 us -> 36.4 us (level)
  no operation moved by 1% of the time
where the time goes in v3:
time: 36.4 us; the launch traced here: 36.3 us
  Pallas kernels  35.5 us (98%)
  local copies, waits for them, and re-layouts  0.8 us (2%)
    pallas_call x1, Pallas kernels, body(): pl.pallas_call(functools.partial(kernel, nx, ny), out_shape=jax.ShapeDtyp...  35.5 us
    unnamed x1, local copies, waits for them, and re-layouts  0.8 us

profile of v3, /device:TPU:1, one launch (start us, length us, event | category | flops | bytes accessed | tf_op | source)
XLA Modules:
  0.0 36.3 jit_solution(10558354964083221871)
XLA Ops:
  0.0 35.5 %shard_map.127 = bf16[2048,128]{1,0:T(8,128)(2,1)S(1)} custom-call(bf16[64,4,8,128]{3,2,1,0:T(8,128)(2,1)} %x_hbm.1, bf16[3,3,3,64,64]{4,3,2,1,0:T(8,128)(2,1)} %w1_hbm.1, bf16[2,2,2,64,128]{4,3,2,1,0:T(8,128)(2,1)} %bitcast.13, bf16[3,3,384,128]{3,2,1,0:T(8,128)(2,1)} %bitcast.11, bf16[3,3,384,128]{3,2,1,0:T(8,128)(2,1)} %bitcast.12, ...), custom_call_target="tpu_custom_call" | custom-call | tf_op jit(solution)/shard_map/pallas_call | solution.py:489
  35.5 0.8 %copy.15 = bf16[64,4,8,128]{3,2,1,0:T(8,128)(2,1)} copy(bf16[64,4,8,128]{3,2,1,0:T(8,128)(2,1)S(1)} %bitcast.10) | data formatting | bytes 1048576

commit v4 on v3

--- a/solution.py
+++ b/solution.py
@@ -364,16 +364,12 @@
         grown = coarse[2 + i, 2 + j].astype(F32) + leaky(part + b3[...])
         final[1 + i, 1 + j] = grown.astype(BF16)
 
-    def meanwhile():
-        start(SKIP, CORNERS)
-        start(SKIP, FACES_X)
-        start(SKIP, FACES_Y)
-        loaded(w3, b3)
-        turn_weights(w3, turned3)
-        loaded(w4, b4, bu)
-        arrange(w4, big4, edge4)
-        column(1, bu)
-        column(2, b4)
+    loaded(w3, b3)
+    turn_weights(w3, turned3)
+    loaded(w4, b4, bu)
+    arrange(w4, big4, edge4)
+    column(1, bu)
+    column(2, b4)
 
     arrived(COARSE, FACES_Y)
     high = CY + 2
@@ -382,7 +378,9 @@
     mine[2] = made[:, 3 * C2 :]
     mine[0] = nn(taken(coarse, (2,), high), weights(turned2, (2,), (1,)))
     mine[3] = nn(taken(coarse, (3,), high), weights(turned2, (3,), (4,)))
-    meanwhile()
+    start(SKIP, CORNERS)
+    start(SKIP, FACES_X)
+    start(SKIP, FACES_Y)
 
     def ring_side(side, first):
         far, near, outs = (0, 1, (1, 2)) if side == 0 else (5, 4, (3, 4))

time: 36.4 us -> 36.4 us (level)
  no operation moved by 1% of the time
where the time goes in v4:
time: 36.4 us; the launch traced here: 36.3 us
  Pallas kernels  35.5 us (98%)
  local copies, waits for them, and re-layouts  0.8 us (2%)
    pallas_call x1, Pallas kernels, body(): pl.pallas_call(functools.partial(kernel, nx, ny), out_shape=jax.ShapeDtyp...  35.5 us
    unnamed x1, local copies, waits for them, and re-layouts  0.8 us

profile of v4, /device:TPU:1, one launch (start us, length us, event | category | flops | bytes accessed | tf_op | source)
XLA Modules:
  0.0 36.3 jit_solution(5611533486097414138)
XLA Ops:
  0.0 35.5 %shard_map.127 = bf16[2048,128]{1,0:T(8,128)(2,1)S(1)} custom-call(bf16[64,4,8,128]{3,2,1,0:T(8,128)(2,1)} %x_hbm.1, bf16[3,3,3,64,64]{4,3,2,1,0:T(8,128)(2,1)} %w1_hbm.1, bf16[2,2,2,64,128]{4,3,2,1,0:T(8,128)(2,1)} %bitcast.13, bf16[3,3,384,128]{3,2,1,0:T(8,128)(2,1)} %bitcast.11, bf16[3,3,384,128]{3,2,1,0:T(8,128)(2,1)} %bitcast.12, ...), custom_call_target="tpu_custom_call" | custom-call | tf_op jit(solution)/shard_map/pallas_call | solution.py:487
  35.5 0.8 %copy.15 = bf16[64,4,8,128]{3,2,1,0:T(8,128)(2,1)} copy(bf16[64,4,8,128]{3,2,1,0:T(8,128)(2,1)S(1)} %bitcast.10) | data formatting | bytes 1048576

commit v5 on v2

--- a/solution.py
+++ b/solution.py
@@ -210,10 +210,11 @@
                 if chunks is None or k in chunks:
                     move.start()
 
-    def arrived(phase, ways):
+    def arrived(phase, ways, chunks=None):
         for way in ways:
-            for move in moves[phase][way]:
-                move.wait_recv()
+            for k, move in enumerate(moves[phase][way]):
+                if chunks is None or k in chunks:
+                    move.wait_recv()
 
     flat[...] = xin[...].astype(F32).reshape(C1 * FX * FY, NZ)
     columns = [(x, y) for x in range(FX) for y in range(FY)]
@@ -385,9 +386,12 @@
     meanwhile()
 
     def ring_side(side, first):
-        arrived(COARSE, ways_of(1 - 2 * side))
-        xs, outs = ((0, 1), (1, 2)) if side == 0 else ((4, 5), (3, 4))
-        made = nn(taken(coarse, xs, high), weights(turned2, xs, outs))
+        far, near, outs = (0, 1, (1, 2)) if side == 0 else (5, 4, (3, 4))
+        arrived(COARSE, ways_of(1 - 2 * side), (side,))
+        o = outs[side]
+        mine[o - 1] = mine[o - 1] + nn(taken(coarse, (far,), high), weights(turned2, (far,), (o,)))
+        arrived(COARSE, ways_of(1 - 2 * side), (1 - side,))
+        made = nn(taken(coarse, (near,), high), weights(turned2, (near,), outs))
         for k, o in enumerate(outs):
             total = mine[o - 1] + made[:, 3 * C2 * k : 3 * C2 * (k + 1)]
             for j in range(high):

time: 36.3 us -> 36.4 us (level)
  no operation moved by 1% of the time
where the time goes in v5:
time: 36.4 us; the launch traced here: 36.3 us
  Pallas kernels  35.5 us (98%)
  local copies, waits for them, and re-layouts  0.8 us (2%)
    pallas_call x1, Pallas kernels, body(): pl.pallas_call(functools.partial(kernel, nx, ny), out_shape=jax.ShapeDtyp...  35.5 us
    unnamed x1, local copies, waits for them, and re-layouts  0.8 us

profile of v5, /device:TPU:1, one launch (start us, length us, event | category | flops | bytes accessed | tf_op | source)
XLA Modules:
  0.0 36.3 jit_solution(8129843356910728548)
XLA Ops:
  0.0 35.5 %shard_map.127 = bf16[2048,128]{1,0:T(8,128)(2,1)S(1)} custom-call(bf16[64,4,8,128]{3,2,1,0:T(8,128)(2,1)} %x_hbm.1, bf16[3,3,3,64,64]{4,3,2,1,0:T(8,128)(2,1)} %w1_hbm.1, bf16[2,2,2,64,128]{4,3,2,1,0:T(8,128)(2,1)} %bitcast.13, bf16[3,3,384,128]{3,2,1,0:T(8,128)(2,1)} %bitcast.11, bf16[3,3,384,128]{3,2,1,0:T(8,128)(2,1)} %bitcast.12, ...), custom_call_target="tpu_custom_call" | custom-call | tf_op jit(solution)/shard_map/pallas_call | solution.py:490
  35.5 0.8 %copy.15 = bf16[64,4,8,128]{3,2,1,0:T(8,128)(2,1)} copy(bf16[64,4,8,128]{3,2,1,0:T(8,128)(2,1)S(1)} %bitcast.10) | data formatting | bytes 1048576
